TPU v7x, 256 devices: a whole 4x4x8 slice. The times are simulated.
256 devices in a mesh: lon: 4 (over x), lat: 64 (over z, y, core).
Axes of the slice: x: 4, y: 4, z: 8, core: 2. Of those that a mesh axis runs over, the one named last changes fastest.
Arguments:
- fields: float32 [2880, 720, 96], P('lat', 'lon'), may hold values from -6 to 6
- weight_one: float32 [8, 2, 96, 96], replicated, may hold values from -0.4375 to 0.4375
- weight_two: float32 [8, 2, 96, 96], replicated, may hold values from -0.4375 to 0.4375
- gate_mask: int32 [256, 2, 8, 360, 96], P(('lon', 'lat')), may hold values 0 or 1
- shrink_mask: int32 [256, 2, 8, 360, 96], P(('lon', 'lat')), may hold values 0 or 1
Outputs:
- tangent_out: float32 [2880, 720, 96], P('lat', 'lon')
All inputs are finite; a program needn't handle non-finite values. No bound on the sum of `gate_mask` or of `shrink_mask` on one device may be relied on, other than what follows from the above.
Results may differ from a plain program's by a relative error of at most 0.00007.
Values sent between devices are 32-bit elements; how exact they have to be, the bound alone decides.
A program may use at most 128 MiB of HBM per device.

v0:
```python
import math

import jax
import jax.numpy as jnp
from jax import lax
from jax.sharding import PartitionSpec as P

W = 720
H = 360
KW = 256


highest = lax.Precision.HIGHEST


def phase_tables(first_idx, second_idx, period):
    product = first_idx[:, None] * second_idx[None, :] % period
    angle = product.astype(jnp.float32) * (2.0 * math.pi / period)
    return (jnp.cos(angle), jnp.sin(angle))


def mix_blocks(real_part, imag_part, weights):
    w_real = weights[:, 0]
    w_imag = weights[:, 1]
    out_real = jnp.einsum("qbmc,bcd->qbmd", real_part, w_real, precision=highest) - jnp.einsum(
        "qbmc,bcd->qbmd", imag_part, w_imag, precision=highest
    )
    out_imag = jnp.einsum("qbmc,bcd->qbmd", imag_part, w_real, precision=highest) + jnp.einsum(
        "qbmc,bcd->qbmd", real_part, w_imag, precision=highest
    )
    return (out_real, out_imag)


def local(fields, weight_one, weight_two, gate_mask, shrink_mask):
    lat_rows, lon_cols, channels = fields.shape
    lon_count = lax.axis_size("lon")
    lat_count = lax.axis_size("lat")
    modes_dev = KW // lon_count
    modes_item = modes_dev // lat_count
    blocks_all = lat_rows * lat_count // H
    lon_place = lax.axis_index("lon")
    lon_global = lon_place * lon_cols + jnp.arange(lon_cols, dtype=jnp.int32)
    scale_lon = 1.0 / math.sqrt(W)
    mode_ids = jnp.arange(lax.axis_size("lon") * modes_dev, dtype=jnp.int32)
    cosine, sine = phase_tables(mode_ids, lon_global, W)
    part_real = jnp.einsum("kw,hwc->khc", cosine, fields, precision=highest)
    part_imag = -jnp.einsum("kw,hwc->khc", sine, fields, precision=highest)
    modes = lax.psum_scatter(
        jnp.concatenate([part_real, part_imag], axis=-1) * scale_lon,
        "lon",
        scatter_dimension=0,
        tiled=True,
    )
    outgoing = modes.reshape(lat_count, modes_item, lat_rows, 2 * channels)
    arrived = lax.all_to_all(outgoing, "lat", split_axis=0, concat_axis=2, tiled=True)[0]
    arrived = arrived.reshape(modes_item, blocks_all, H, 2 * channels)
    lat_ids = jnp.arange(H, dtype=jnp.int32)
    cos_lat, sin_lat = phase_tables(lat_ids, lat_ids, H)
    cos_lat = cos_lat / math.sqrt(H)
    sin_lat = sin_lat / math.sqrt(H)
    in_real = arrived[..., :channels]
    in_imag = arrived[..., channels:]
    spec_real = jnp.einsum("mh,qbhc->qbmc", cos_lat, in_real, precision=highest) + jnp.einsum(
        "mh,qbhc->qbmc", sin_lat, in_imag, precision=highest
    )
    spec_imag = jnp.einsum("mh,qbhc->qbmc", cos_lat, in_imag, precision=highest) - jnp.einsum(
        "mh,qbhc->qbmc", sin_lat, in_real, precision=highest
    )
    gates = gate_mask.astype(jnp.float32)
    shrink = shrink_mask.astype(jnp.float32)
    hid_real, hid_imag = mix_blocks(spec_real, spec_imag, weight_one)
    hid_real = hid_real * gates[:, 0]
    hid_imag = hid_imag * gates[:, 1]
    mix_real, mix_imag = mix_blocks(hid_real, hid_imag, weight_two)
    mix_real = mix_real * shrink[:, 0]
    mix_imag = mix_imag * shrink[:, 1]
    band_real = jnp.einsum("mh,qbmc->qbhc", cos_lat, mix_real, precision=highest) - jnp.einsum(
        "mh,qbmc->qbhc", sin_lat, mix_imag, precision=highest
    )
    band_imag = jnp.einsum("mh,qbmc->qbhc", cos_lat, mix_imag, precision=highest) + jnp.einsum(
        "mh,qbmc->qbhc", sin_lat, mix_real, precision=highest
    )
    leaving = jnp.concatenate([band_real, band_imag], axis=-1).reshape(
        modes_item, lat_count, lat_rows, 2 * channels
    )
    returned = lax.all_to_all(leaving, "lat", split_axis=1, concat_axis=0, tiled=True).reshape(
        modes_dev, lat_rows, 2 * channels
    )
    piece = lax.all_gather(returned, "lon", axis=0, tiled=True)
    mode_ids = jnp.arange(piece.shape[0], dtype=jnp.int32)
    factor = jnp.where(mode_ids == 0, 1.0, 2.0).astype(jnp.float32) * scale_lon
    cosine, sine = phase_tables(mode_ids, lon_global, W)
    cosine = cosine * factor[:, None]
    sine = sine * factor[:, None]
    return jnp.einsum("kw,khc->hwc", cosine, piece[..., :channels], precision=highest) - jnp.einsum(
        "kw,khc->hwc", sine, piece[..., channels:], precision=highest
    )


def solution(mesh):
    in_specs = (
        P("lat", "lon", None),
        P(),
        P(),
        P(("lon", "lat"), None, None, None, None),
        P(("lon", "lat"), None, None, None, None),
    )
    out_specs = P("lat", "lon", None)
    return jax.shard_map(local, mesh=mesh, in_specs=in_specs, out_specs=out_specs, check_vma=False)
```

profile of v0, /device:TPU:1, one launch (start us, length us, event | category | flops | bytes accessed | tf_op | source)
XLA Modules:
  0.0 556.6 jit_solution(14436433692685589657)
XLA Ops:
  6.5 0.0 reduce-scatter.2.cloned.1.call-start
  6.5 0.0 copy-start
  6.5 11.2 %convolution_negate_fusion = f32[256,45,96]{0,2,1:T(8,128)S(1)} fusion(f32[45,180,96]{2,1,0:T(8,128)} %param.5, s32[180]{0:T(256)S(1)} %iota_add_fusion), kind=kOutput, calls=%fused_computation.7 | convolution fusion | flops 2390307840 | bytes 7534800 | tf_op jit(solution)/shard_map/kw,hwc->khc/dot_general | solution.py:47
  17.8 0.0 copy-done
  17.8 9.5 %fusion.96 = f32[256,45,96]{0,2,1:T(8,128)S(1)} fusion(f32[45,180,96]{2,1,0:T(8,128)S(1)} %copy-done, s32[180]{0:T(256)S(1)} %iota_add_fusion), kind=kOutput, calls=%fused_computation.107 | convolution fusion | flops 2389201920 | bytes 7534800 | tf_op jit(solution)/shard_map/kw,hwc->khc/dot_general | solution.py:46
  27.3 4.7 maximum_multiply_fusion
  32.0 12.6 %copy.19 = f32[256,45,192]{2,1,0:T(8,128)} copy(f32[256,45,192]{0,2,1:T(8,128)} %maximum_multiply_fusion) | data formatting | bytes 17694720 | tf_op jit(solution)/shard_map/mul | solution.py:49
  44.6 0.0 reduce-scatter.2.cloned.1.call-update
  44.6 121.0 %reduce-scatter.2.cloned.1.call-done = f32[64,45,192]{2,1,0:T(8,128)} async-done(((f32[256,45,192]{2,1,0:T(8,128)}), f32[64,45,192]{2,1,0:T(8,128)}) %reduce-scatter.2.cloned.1.call-update) | async-done | bytes 2211856 | tf_op jit(solution)/shard_map/reduce_scatter | solution.py:48
  165.6 6.5 %copy.20 = f32[64,1,45,192]{3,1,2,0:T(1,128)} copy(f32[64,1,45,192]{3,2,0,1:T(8,128)} %bitcast.182) | data formatting | bytes 4423680 | tf_op jit(solution)/shard_map/reshape | solution.py:54
  172.1 10.6 %all-to-all-start = ((f32[64,1,45,192]{3,1,2,0:T(1,128)}), f32[64,1,45,192]{3,1,2,0:T(1,128)S(1)}, u32[]{:S(2)}, u32[]{:S(2)}) async-start(f32[64,1,45,192]{3,1,2,0:T(1,128)} %copy.20), calls=%async_computation.1 | async-start | bytes 5898240 | tf_op jit(solution)/shard_map/all_to_all | solution.py:55
  182.8 0.3 all-gather.3.cloned.1.call-start
  183.1 0.0 copy-start.5
  183.1 3.4 convert_element_type.29
  186.5 0.0 copy-done.5
  186.5 1.6 convert_element_type.30
  188.1 63.0 %all-to-all-done = f32[64,1,45,192]{3,1,2,0:T(1,128)S(1)} async-done(((f32[64,1,45,192]{3,1,2,0:T(1,128)}), f32[64,1,45,192]{3,1,2,0:T(1,128)S(1)}, u32[]{:S(2)}, u32[]{:S(2)}) %all-to-all-start) | async-done | bytes 2211872 | tf_op jit(solution)/shard_map/all_to_all | solution.py:55
  251.1 4.0 fusion.172
  255.2 6.8 %fusion.34 = f32[8,96,360]{2,1,0:T(8,128)S(1)} fusion(f32[8,360,96]{2,1,0:T(8,128)S(1)} %bitcast.176), kind=kOutput, calls=%fused_computation.49 | convolution fusion | flops 1195689600 | bytes 2211840 | tf_op jit(solution)/shard_map/mh,qbhc->qbmc/dot_general | solution.py:63
  261.9 7.1 %fusion.32 = f32[8,96,360]{2,1,0:T(8,128)S(1)} fusion(f32[8,360,96]{2,1,0:T(8,128)S(1)} %bitcast.178), kind=kOutput, calls=%fused_computation.47 | convolution fusion | flops 1195689600 | bytes 2211840 | tf_op jit(solution)/shard_map/mh,qbhc->qbmc/dot_general | solution.py:66
  269.1 6.9 %fusion.7 = f32[8,360,96]{1,2,0:T(8,128)S(1)} fusion(f32[8,96,360]{2,1,0:T(8,128)S(1)} %fusion.34, f32[8,360,96]{2,1,0:T(8,128)S(1)} %bitcast.179), kind=kOutput, calls=%fused_computation.17 | convolution fusion | flops 1195966080 | bytes 3317760 | tf_op jit(solution)/shard_map/mh,qbhc->qbmc/dot_general | solution.py:63
  276.0 0.0 copy-start.3
  276.0 6.8 %fusion.6 = f32[8,360,96]{1,2,0:T(8,128)S(1)} fusion(f32[8,96,360]{2,1,0:T(8,128)S(1)} %fusion.32, f32[8,360,96]{2,1,0:T(8,128)S(1)} %bitcast.177), kind=kOutput, calls=%fused_computation.15 | convolution fusion | flops 1195966080 | bytes 3317760 | tf_op jit(solution)/shard_map/mh,qbhc->qbmc/dot_general | solution.py:66
  282.8 0.0 copy-done.3
  282.8 1.2 fusion.49
  284.1 0.0 copy-start.2
  284.1 1.2 fusion.47
  285.3 0.4 copy-done.2
  285.7 1.3 fusion.21
  287.0 0.0 copy-start.4
  287.0 1.5 fusion.19
  288.5 0.0 copy-done.4
  288.5 1.2 fusion.43
  289.8 0.0 copy-start.1
  289.8 1.2 fusion.41
  291.0 0.4 copy-done.1
  291.4 1.3 fusion.17
  292.7 4.6 fusion.30
  297.3 1.3 fusion.15
  298.6 4.9 fusion.28
  303.5 4.6 fusion.12
  308.1 4.5 fusion.13
  312.6 1.6 pad_maximum_fusion
  314.2 7.5 %copy.27 = f32[1,8,360,192]{3,0,2,1:T(1,128)S(1)} copy(f32[1,8,360,192]{2,3,1,0:T(8,128)} %pad_maximum_fusion) | data formatting | bytes 4423680 | tf_op jit(solution)/shard_map/concatenate | solution.py:83
  321.7 75.9 %all_to_all.8 = f32[1,64,45,192]{3,0,2,1:T(1,128)} all-to-all(f32[1,64,45,192]{3,0,2,1:T(1,128)S(1)} %bitcast.181), channel_id=1, replica_groups=mesh['lon'=4,'lat'=64] {'lat'}, dimensions={1} | all-to-all | bytes 4423680 | tf_op jit(solution)/shard_map/all_to_all | solution.py:86
  397.6 0.0 all-gather.3.cloned.1.call-update
  397.6 109.8 %all-gather.3.cloned.1.call-done = f32[1,256,45,192]{3,0,2,1:T(1,128)} async-done(((f32[1,64,45,192]{3,0,2,1:T(1,128)}), f32[1,256,45,192]{3,0,2,1:T(1,128)}) %all-gather.3.cloned.1.call-update) | async-done | bytes 8847376 | tf_op jit(solution)/shard_map/all_gather | solution.py:89
  507.4 24.4 %copy.28 = f32[1,256,45,192]{1,3,2,0:T(8,128)} copy(f32[1,256,45,192]{3,0,2,1:T(1,128)} %all-gather.3.cloned.1.call-done) | data formatting | bytes 17694720 | tf_op jit(solution)/shard_map/all_gather | solution.py:89
  531.8 8.1 %fusion = f32[45,96,180]{1,2,0:T(8,128)S(1)} fusion(f32[256,45,192]{0,2,1:T(8,128)} %bitcast.174, f32[256]{0:T(256)S(1)} %fusion.127, s32[180]{0:T(256)S(1)} %iota_add_fusion), kind=kOutput, calls=%fused_computation.1 | convolution fusion | flops 2389248000 | bytes 7535824 | tf_op jit(solution)/shard_map/kw,khc->hwc/dot_general | solution.py:95
  539.9 9.7 %subtract_bitcast_fusion = f32[45,180,96]{2,1,0:T(8,128)} fusion(f32[45,96,180]{1,2,0:T(8,128)S(1)} %fusion, f32[256,45,192]{0,2,1:T(8,128)} %bitcast.175, f32[256]{0:T(256)S(1)} %fusion.127, s32[180]{0:T(256)S(1)} %iota_add_fusion), kind=kOutput, calls=%fused_computation.5 | convolution fusion | flops 2390025728 | bytes 10646224 | tf_op jit(solution)/shard_map/kw,khc->hwc/dot_general | solution.py:95
  (2 shorter events, 0.0 us)
Async XLA Ops:
  6.5 159.1 %reduce-scatter.2.cloned.1.call-start = ((), (), s32[]{:S(2)}) async-start(), calls=%async_computation.3 | async-start | bytes 15728640 | tf_op jit(solution)/shard_map/reduce_scatter | solution.py:48
  6.5 11.2 %copy-start = (f32[45,180,96]{2,1,0:T(8,128)S(1)}, f32[45,180,96]{2,1,0:T(8,128)}, u32[]{:S(2)}) copy-start(f32[45,180,96]{2,1,0:T(8,128)} %param.5) | copy-start | bytes 9331204
  172.1 79.0 %all-to-all-start = ((f32[64,1,45,192]{3,1,2,0:T(1,128)}), f32[64,1,45,192]{3,1,2,0:T(1,128)S(1)}, u32[]{:S(2)}, u32[]{:S(2)}) async-start(f32[64,1,45,192]{3,1,2,0:T(1,128)} %copy.20), calls=%async_computation.1 | async-start | bytes 5898240 | tf_op jit(solution)/shard_map/all_to_all | solution.py:55
  182.8 324.6 %all-gather.3.cloned.1.call-start = ((), (), s32[]{:S(2)}) async-start(), calls=%async_computation.4 | async-start | bytes 14745600 | tf_op jit(solution)/shard_map/all_gather | solution.py:89
  183.1 3.5 copy-start.5
  276.0 6.8 %copy-start.3 = (f32[8,2,96,96]{3,2,1,0:T(8,128)S(1)}, f32[8,2,96,96]{3,2,1,0:T(8,128)}, u32[]{:S(2)}) copy-start(f32[8,2,96,96]{3,2,1,0:T(8,128)} %param.6) | copy-start | bytes 1769476
  284.1 1.7 copy-start.2
  287.0 1.5 copy-start.4
  289.8 1.7 copy-start.1
Sparse Core Ops, SparseCore 0:
  44.7 120.8 reduce-scatter.1
  397.7 109.6 all-gather.2
where the time goes:
time: 566 us; the launch traced here: 557 us
  waiting for transfers between devices  294 us (52%)
  matrix products  94.9 us (17%)
  blocking collectives  75.9 us (13%)
  local copies, waits for them, and re-layouts  56 us (10%)
  between operations  13.8 us (2%)
  other arithmetic  11.3 us (2%)
  starting transfers between devices  10.9 us (2%)
    reduce_scatter x1, waiting for transfers between devices, local(): lax.psum_scatter(jnp.concatenate([part_real, part_imag], axis=-1) * scale...  121 us
    all_gather x1, waiting for transfers between devices, local(): piece = lax.all_gather(returned, 'lon', axis=0, tiled=True)  110 us
    all_to_all x1, blocking collectives, local(): lax.all_to_all(leaving, 'lat', split_axis=1, concat_axis=0, tiled=True)  75.9 us
    all_to_all x1, waiting for transfers between devices, local(): lax.all_to_all(outgoing, 'lat', split_axis=0, concat_axis=2, tiled=True)[0]  63 us
    all_gather x1, local copies, waits for them, and re-layouts, local(): piece = lax.all_gather(returned, 'lon', axis=0, tiled=True)  24.4 us
    mul x1, local copies, waits for them, and re-layouts, local(): jnp.concatenate([part_real, part_imag], axis=-1) * scale_lon  12.6 us
  transfers between devices with their start and end apart: 3, of which 3 were waited for; matrix products, arithmetic and copies ran while one was open for 1% of the time, Pallas kernels for 0%

commit v1 on v0

v1 whole, which is shorter than its diff:
```python
import functools
import math

import jax
import jax.numpy as jnp
import ml_dtypes
import numpy as np
from jax import lax
from jax.experimental import pallas as pl
from jax.experimental.pallas import tpu as pltpu
from jax.sharding import PartitionSpec as P

MESH = pl.DeviceIdType.MESH
W = 720
H = 360
C = 96
KW = 256
NB = 8
NX = 4
NS = 32
HL = 45
WL = 180
WP = 184
KP = 192
RP = 12
NG = 3
MP = 384
NT = 9
MSG = NT * 8
F32 = jnp.float32
BF16 = jnp.bfloat16


def split_table(table):
    high = table.astype(ml_dtypes.bfloat16)
    low = (table - high.astype(np.float64)).astype(ml_dtypes.bfloat16)
    return np.stack([high, low])


@functools.lru_cache(None)
def tables():
    half = np.arange(2)[:, None, None, None]
    dest = np.arange(NS)[None, :, None, None]
    part = np.arange(2)[None, None, :, None]
    four = np.arange(4)[None, None, None, :]
    mode = 64 * (dest // 8) + 8 * (4 * half + four) + dest % 8 + 0 * part
    part = part + 0 * mode
    mode, part = mode.reshape(2, 256), part.reshape(2, 256)

    def wave(angle, which):
        return np.where(which == 0, np.cos(angle), -np.sin(angle))

    depth = np.arange(NX * KP)
    lon = 180 * (depth // KP) + depth % KP
    angle = 2 * math.pi / W * (mode[:, :, None] * lon % W)
    forward = wave(angle, part[:, :, None]) / math.sqrt(W) * (depth % KP < WL)

    rows = np.arange(NX * WP)
    lon = 180 * (rows // WP) + rows % WP
    angle = 2 * math.pi / W * (mode[:, None, :] * lon[:, None] % W)
    factor = np.where(mode == 0, 1.0, 2.0)[:, None, :]
    back = wave(angle, part[:, None, :]) * factor / math.sqrt(W) * (rows % WP < WL)[:, None]

    place = np.arange(MP)
    source = place % NS
    local_row = RP * (source // 8) + place // NS
    lat = HL * (source % 8) + local_row
    m = np.arange(MP)
    angle = 2 * math.pi / H * (m[:, None] * lat[None, :] % H)
    keep = (m < H)[:, None] * (local_row < HL)[None, :] / math.sqrt(H)
    cosine, sine = np.cos(angle) * keep, np.sin(angle) * keep
    lat_fwd = np.block([[cosine, sine], [-sine, cosine]])
    lat_back = lat_fwd.T
    return tuple(split_table(t) for t in (forward, lat_fwd, lat_back, back))


def high_low(value):
    high = value.astype(BF16)
    return high, (value - high.astype(F32)).astype(BF16)


def dot3(a, b, dims=((1,), (0,))):
    def one(p, q):
        return lax.dot_general(p, q, (dims, ((), ())), preferred_element_type=F32)

    return one(a[0], b[0]) + (one(a[0], b[1]) + one(a[1], b[0]))


NT_DIMS = ((1,), (1,))


def kernel(
    fields, w1, w2, gate, shrink, t_fwd, t_lat, t_bck, t_inv, out,
    fv, xs, xr, xhi, xlo, ys, yr, cs, cr, osn, orc, ov, gv, sv, wv, wt,
    vfwd, vlat, vbck, vinv, shi, slo, phi, plo, hhi, hlo, mhi, mlo,
    s_load, s_out, sa, ra, sb, rb, sc, rc, sd, rd, sm, rm,
):
    x = lax.axis_index("lon")
    t = lax.axis_index("lat")
    z = t // 8
    yc = t % 8
    y = yc // 2
    core = yc % 2
    me = x * 8 + yc
    zh = z // 4
    zl = z % 4

    load_fields = pltpu.make_async_copy(fields, fv.at[pl.ds(0, HL)], s_load.at[0])
    load_fields.start()
    loads = [
        pltpu.make_async_copy(w1.at[z], wv.at[0], s_load.at[1]),
        pltpu.make_async_copy(w2.at[z], wv.at[1], s_load.at[2]),
        pltpu.make_async_copy(t_fwd, vfwd, s_load.at[3]),
        pltpu.make_async_copy(t_lat, vlat, s_load.at[4]),
        pltpu.make_async_copy(t_bck, vbck, s_load.at[5]),
        pltpu.make_async_copy(t_inv, vinv, s_load.at[6]),
    ]
    for copy in loads:
        copy.start()

    def plane_peer(i):
        dx, r = i % 4, i // 4
        px = (x + dx) % 4
        py = (y + r // 2 + dx) % 4
        pc = (core + r + dx) % 2
        return px * 8 + py * 2 + pc

    def plane_id(d):
        return (d // 8, z * 8 + d % 8)

    barrier = pltpu.get_barrier_semaphore()

    @pl.loop(1, NS)
    def _(i):
        pl.semaphore_signal(barrier, inc=1, device_id=plane_id(plane_peer(i)), device_id_type=MESH)

    @pl.loop(1, NB)
    def _(i):
        pl.semaphore_signal(barrier, inc=1, device_id=(x, ((z + i) % 8) * 8 + yc), device_id_type=MESH)

    fv[HL : RP * NX] = jnp.zeros((RP * NX - HL, WL, C), F32)
    hhi[...] = jnp.zeros_like(hhi)
    hlo[...] = jnp.zeros_like(hlo)
    mhi[...] = jnp.zeros_like(mhi)
    mlo[...] = jnp.zeros_like(mlo)

    def pack(g, dx, put):
        base = RP * ((x + dx) % 4) + 4 * g
        last = fv[base + 3]
        for j in range(3):
            put(j, jnp.concatenate([fv[base + j], last[:, 32 * j : 32 * j + 32]], axis=1))

    def pack_group(g):
        for dx in (2, 1, 3):

            def put(j, value):
                xs[g, dx - 1, j, WP - 8 : WP] = jnp.zeros((8, 128), F32)
                xs[g, dx - 1, j, 0:WL] = value

            pack(g, dx, put)

    def send_group(g):
        for dx in (2, 1, 3):
            pltpu.make_async_remote_copy(
                src_ref=xs.at[g, dx - 1], dst_ref=xr.at[g, x], send_sem=sa.at[g], recv_sem=ra.at[g],
                device_id=((x + dx) % 4, t), device_id_type=MESH,
            ).start()

    load_fields.wait()
    pack_group(0)
    pl.semaphore_wait(barrier, NS - 1 + NB - 1)
    send_group(0)

    def send_mask(src, dst, b, which):
        pltpu.make_async_remote_copy(
            src_ref=src.at[0, :, b], dst_ref=dst.at[z], send_sem=sm, recv_sem=rm.at[which],
            device_id=(x, b * 8 + yc), device_id_type=MESH,
        ).start()

    pltpu.make_async_copy(gate.at[0, :, z], gv.at[z], rm.at[0]).start()
    pltpu.make_async_copy(shrink.at[0, :, z], sv.at[z], rm.at[0]).start()
    for i in range(1, 4):
        send_mask(gate, gv, 4 * zh + (zl + i) % 4, 0)
        send_mask(shrink, sv, 4 * zh + (zl + i) % 4, 0)
    for i in range(4):
        send_mask(gate, gv, 4 * (1 - zh) + (zl + i) % 4, 1)
    for i in range(4):
        send_mask(shrink, sv, 4 * (1 - zh) + (zl + i) % 4, 2)

    for g in range(1, NG):
        pack_group(g)
        send_group(g)

    for g in range(NG):

        def put(j, value):
            xr[g, x, j, WP - 8 : WP] = jnp.zeros((8, 128), F32)
            xr[g, x, j, 0:WL] = value

        pack(g, 0, put)

    for copy in loads:
        copy.wait()
    for which in range(2):
        wt[...] = jnp.zeros((256, 256), F32)
        wt[0:C, 0:C] = wv[which, 0]
        wt[0:C, 128 : 128 + C] = wv[which, 1]
        wt[128 : 128 + C, 0:C] = -wv[which, 1]
        wt[128 : 128 + C, 128 : 128 + C] = wv[which, 0]
        turned = wt[...].T
        high, low = high_low(turned)
        if which == 0:
            w1t = (high, low)
        else:
            w2t = (high, low)

    for g in range(NG):
        pltpu.make_async_copy(xr.at[g, pl.ds(0, 3)], xr.at[g, pl.ds(0, 3)], ra.at[g]).wait()
        for s in range(NX):
            for j in range(3):
                value = jnp.concatenate([xr[g, s, j], jnp.zeros((KP - WP, 128), F32)], axis=0)
                high, low = high_low(value)
                xhi[KP * s : KP * s + KP, 128 * j : 128 * j + 128] = high
                xlo[KP * s : KP * s + KP, 128 * j : 128 * j + 128] = low
        for turn in range(2):
            half = (zh + turn) % 2
            modes = dot3((vfwd[0, half], vfwd[1, half]), (xhi[...], xlo[...]))
            for j in range(3):
                tile = 8 * (3 * g + j)
                ys[half, :, tile : tile + 8, :] = modes[:, 128 * j : 128 * j + 128].reshape(NS, 8, 128)
            if g == NG - 1:
                own = pltpu.make_async_copy(ys.at[half, me], yr.at[half, me], rb.at[half])
                own.start()

                @pl.loop(1, NS)
                def _(i):
                    d = plane_peer(i)
                    pltpu.make_async_remote_copy(
                        src_ref=ys.at[half, d], dst_ref=yr.at[half, me], send_sem=sb.at[half], recv_sem=rb.at[half],
                        device_id=plane_id(d), device_id_type=MESH,
                    ).start()

    yflat = yr.reshape(2, NS * MSG, 128)
    cflat = cs.reshape(2, NS * MSG, 128)
    for turn in range(2):
        half = (zh + turn) % 2
        pltpu.make_async_copy(yr.at[half], yr.at[half], rb.at[half]).wait()
        if turn == 0:
            pltpu.make_async_copy(gv, gv, rm.at[0]).wait()
        else:
            pltpu.make_async_copy(gv.at[pl.ds(0, 4)], gv.at[pl.ds(0, 4)], rm.at[1]).wait()
            pltpu.make_async_copy(sv.at[pl.ds(0, 4)], sv.at[pl.ds(0, 4)], rm.at[2]).wait()

        @pl.loop(0, 2)
        def _(pair):
            for pos in range(2):
                for ri in range(2):
                    for g in range(NG):
                        tiles = [
                            yflat[half, pl.ds((3 * g + j) * 8 + ri * 4 + 2 * pair + pos, NS, stride=MSG), :]
                            for j in range(3)
                        ]
                        last = jnp.concatenate([v[:, C:] for v in tiles] + [tiles[0][:, C:]], axis=1)
                        for r, value in enumerate(tiles + [last]):
                            high, low = high_low(value)
                            at = ri * MP + (g * 4 + r) * NS
                            shi[at : at + NS, 128 * pos : 128 * pos + 128] = high
                            slo[at : at + NS, 128 * pos : 128 * pos + 128] = low
            spec = dot3((vlat[0], vlat[1]), (shi[...], slo[...]))
            for pos in range(2):
                for ri in range(2):
                    high, low = high_low(spec[MP * ri : MP * ri + MP, 128 * pos : 128 * pos + 128])
                    phi[pos, :, 128 * ri : 128 * ri + 128] = high
                    plo[pos, :, 128 * ri : 128 * ri + 128] = low
            for pos in range(2):
                q = 4 * half + 2 * pair + pos
                hid = dot3(w1t, (phi[pos], plo[pos]), NT_DIMS)
                for ri in range(2):
                    high, low = high_low(hid[128 * ri : 128 * ri + C, 0:H] * gv[q, ri].astype(F32))
                    hhi[128 * ri : 128 * ri + C, 0:H] = high
                    hlo[128 * ri : 128 * ri + C, 0:H] = low
                mix = dot3(w2t, (hhi[...], hlo[...]))
                for ri in range(2):
                    high, low = high_low(mix[128 * ri : 128 * ri + C, 0:H] * sv[q, ri].astype(F32))
                    mhi[128 * pos : 128 * pos + C, MP * ri : MP * ri + H] = high
                    mlo[128 * pos : 128 * pos + C, MP * ri : MP * ri + H] = low
            band = dot3((vbck[0], vbck[1]), (mhi[...], mlo[...]), NT_DIMS)
            for pos in range(2):
                for ri in range(2):
                    for g in range(NG):
                        at = ri * MP + g * 4 * NS
                        rows = [
                            band[at + r * NS : at + r * NS + NS, 128 * pos : 128 * pos + 128] for r in range(4)
                        ]
                        for j in range(3):
                            value = jnp.concatenate([rows[j][:, 0:C], rows[3][:, 32 * j : 32 * j + 32]], axis=1)
                            start = (3 * g + j) * 8 + ri * 4 + 2 * pair + pos
                            cflat[half, pl.ds(start, NS, stride=MSG), :] = value

        pltpu.make_async_copy(cs.at[half, me], cr.at[half, me], rc.at[half]).start()

        @pl.loop(1, NS)
        def _(i):
            d = plane_peer(i)
            pltpu.make_async_remote_copy(
                src_ref=cs.at[half, d], dst_ref=cr.at[half, me], send_sem=sc.at[half], recv_sem=rc.at[half],
                device_id=plane_id(d), device_id_type=MESH,
            ).start()

    for half in range(2):
        pltpu.make_async_copy(cr.at[half], cr.at[half], rc.at[half]).wait()
    for g in range(NG):
        for j in range(3):
            tile = 8 * (3 * g + j)
            for half in range(2):
                high, low = high_low(cr[half, :, tile : tile + 8, :].reshape(256, 128))
                xhi[256 * half : 256 * half + 256, 128 * j : 128 * j + 128] = high
                xlo[256 * half : 256 * half + 256, 128 * j : 128 * j + 128] = low
        whole = None
        for half in range(2):
            rows = slice(256 * half, 256 * half + 256)
            term = dot3((vinv[0, half], vinv[1, half]), (xhi[rows], xlo[rows]))
            whole = term if whole is None else whole + term
        for s in range(NX):
            for j in range(3):
                osn[g, s, j] = whole[WP * s : WP * s + WP, 128 * j : 128 * j + 128]
        pltpu.make_async_copy(osn.at[g, x], orc.at[g, x], rd.at[g]).start()
        for dx in (2, 1, 3):
            to = (x + dx) % 4
            pltpu.make_async_remote_copy(
                src_ref=osn.at[g, to], dst_ref=orc.at[g, x], send_sem=sd.at[g], recv_sem=rd.at[g],
                device_id=(to, t), device_id_type=MESH,
            ).start()

    stores = []
    for g in range(NG):
        pltpu.make_async_copy(orc.at[g], orc.at[g], rd.at[g]).wait()
        for s in range(NX):
            tiles = [orc[g, s, j] for j in range(3)]
            base = RP * s + 4 * g
            count = min(4, HL - base)
            for r in range(min(3, count)):
                ov[base + r] = tiles[r][0:WL, 0:C]
            if count == 4:
                ov[base + 3] = jnp.concatenate([v[0:WL, C:] for v in tiles], axis=1)
            copy = pltpu.make_async_copy(ov.at[pl.ds(base, count)], out.at[pl.ds(base, count)], s_out.at[g, s])
            copy.start()
            stores.append(copy)

    for copy in stores:
        copy.wait()
    for g in range(NG):
        pltpu.make_async_copy(xs.at[g], xs.at[g], sa.at[g]).wait()
        pltpu.make_async_copy(xs.at[g], xs.at[g], sd.at[g]).wait()
    for half in range(2):
        sent = ys.at[half, pl.ds(0, NS - 1)]
        pltpu.make_async_copy(sent, sent, sb.at[half]).wait()
        pltpu.make_async_copy(sent, sent, sc.at[half]).wait()
    pltpu.make_async_copy(gv.at[pl.ds(0, 7)], gv.at[pl.ds(0, 7)], sm).wait()
    pltpu.make_async_copy(gv.at[pl.ds(0, 7)], gv.at[pl.ds(0, 7)], sm).wait()


def local(fields, weight_one, weight_two, gate_mask, shrink_mask):
    gate = jnp.swapaxes(gate_mask, 3, 4)
    shrink = jnp.swapaxes(shrink_mask, 3, 4)
    consts = [jnp.asarray(t) for t in tables()]
    dma = pltpu.SemaphoreType.DMA
    any_spec = pl.BlockSpec(memory_space=pl.ANY)
    vm = pltpu.VMEM
    scratch = [
        vm((RP * NX, WL, C), F32),
        vm((NG, 3, 3, WP, 128), F32),
        vm((NG, NX, 3, WP, 128), F32),
        vm((NX * KP, 384), BF16),
        vm((NX * KP, 384), BF16),
        vm((2, NS, MSG, 128), F32),
        vm((2, NS, MSG, 128), F32),
        vm((2, NS, MSG, 128), F32),
        vm((2, NS, MSG, 128), F32),
        vm((NG, NX, 3, WP, 128), F32),
        vm((NG, NX, 3, WP, 128), F32),
        vm((HL, WL, C), F32),
        vm((NB, 2, C, H), jnp.int32),
        vm((NB, 2, C, H), jnp.int32),
        vm((2, 2, C, C), F32),
        vm((256, 256), F32),
        vm((2, 2, 256, NX * KP), BF16),
        vm((2, 2 * MP, 2 * MP), BF16),
        vm((2, 2 * MP, 2 * MP), BF16),
        vm((2, 2, NX * WP, 256), BF16),
        vm((2 * MP, 256), BF16),
        vm((2 * MP, 256), BF16),
        vm((2, MP, 256), BF16),
        vm((2, MP, 256), BF16),
        vm((256, MP), BF16),
        vm((256, MP), BF16),
        vm((256, 2 * MP), BF16),
        vm((256, 2 * MP), BF16),
        dma((7,)),
        dma((NG, NX)),
        dma((NG,)),
        dma((NG,)),
        dma((2,)),
        dma((2,)),
        dma((2,)),
        dma((2,)),
        dma((NG,)),
        dma((NG,)),
        dma,
        dma((3,)),
    ]
    return pl.pallas_call(
        kernel,
        name="afno_tangent",
        out_shape=jax.ShapeDtypeStruct((HL, WL, C), F32),
        in_specs=[any_spec] * 9,
        out_specs=any_spec,
        scratch_shapes=scratch,
        compiler_params=pltpu.CompilerParams(
            collective_id=0, has_side_effects=True, vmem_limit_bytes=62 * 2**20
        ),
    )(fields, weight_one, weight_two, gate, shrink, *consts)


def solution(mesh):
    in_specs = (
        P("lat", "lon", None),
        P(),
        P(),
        P(("lon", "lat"), None, None, None, None),
        P(("lon", "lat"), None, None, None, None),
    )
    out_specs = P("lat", "lon", None)
    return jax.shard_map(local, mesh=mesh, in_specs=in_specs, out_specs=out_specs, check_vma=False)
```

time: 566 us -> 189 us (0.33); the launches traced: 557 us -> 188 us
  waiting for transfers between devices: 294 us -> 0 us
  Pallas kernels: 0 us -> 184 us
  matrix products: 94.9 us -> 0 us
  blocking collectives: 75.9 us -> 0 us
  local copies, waits for them, and re-layouts: 56 us -> 4.5 us
  between operations: 13.8 us -> 0.01 us
  other arithmetic: 11.3 us -> 0 us
  starting transfers between devices: 10.9 us -> 0 us
    pallas_call x0 -> x1, Pallas kernels: none -> 184 us  [local(): pl.pallas_call(kernel, name='afno_tangent', out_shape=jax.ShapeDtypeStruc...]
    reduce_scatter x1 -> x0, waiting for transfers between devices: 121 us -> none  [local(): lax.psum_scatter(jnp.concatenate([part_real, part_imag], axis=-1) * scale...]
    all_gather x1 -> x0, waiting for transfers between devices: 110 us -> none  [local(): piece = lax.all_gather(returned, 'lon', axis=0, tiled=True)]
    dot_general x20 -> x0, matrix products: 94.9 us -> none  [the longest x1 11.2 us: local(): part_imag = -jnp.einsum('kw,hwc->khc', sine, fields, precision=highest)]
    all_to_all x1 -> x0, blocking collectives: 75.9 us -> none  [local(): lax.all_to_all(leaving, 'lat', split_axis=1, concat_axis=0, tiled=True)]
    all_to_all x1 -> x0, waiting for transfers between devices: 63 us -> none  [local(): lax.all_to_all(outgoing, 'lat', split_axis=0, concat_axis=2, tiled=True)[0]]
    all_gather x1 -> x0, local copies, waits for them, and re-layouts: 24.4 us -> none  [local(): piece = lax.all_gather(returned, 'lon', axis=0, tiled=True)]
    mul x1 -> x0, local copies, waits for them, and re-layouts: 12.6 us -> none  [local(): jnp.concatenate([part_real, part_imag], axis=-1) * scale_lon]
  transfers between devices with their start and end apart: 3 -> 0, of which waited for: 3 -> 0; matrix products, arithmetic and copies ran while one was open for 1% -> 0% of each run, Pallas kernels for 0% -> 0%
where the time goes in v1:
time: 189 us; the launch traced here: 188 us
  Pallas kernels  184 us (97%)
  local copies, waits for them, and re-layouts  4.5 us (2%)
    pallas_call x1, Pallas kernels, local(): pl.pallas_call(kernel, name='afno_tangent', out_shape=jax.ShapeDtypeStruc...  184 us
    unnamed x1, local copies, waits for them, and re-layouts  4.5 us

profile of v1, /device:TPU:1, one launch (start us, length us, event | category | flops | bytes accessed | tf_op | source)
XLA Modules:
  0.0 188.4 jit_solution(11821987687046664049)
XLA Ops:
  0.0 183.9 %afno_tangent.1 = f32[45,180,96]{2,1,0:T(8,128)} custom-call(f32[45,180,96]{2,1,0:T(8,128)} %fields.1, f32[8,2,96,96]{3,2,1,0:T(8,128)} %w1.1, f32[8,2,96,96]{3,2,1,0:T(8,128)} %w2.1, s32[1,2,8,96,360]{4,3,2,1,0:T(8,128)} %bitcast.2, s32[1,2,8,96,360]{4,3,2,1,0:T(8,128)} %bitcast.3, bf16[2,2,256,768]{3,2,1,0:T(8,128)(2,1)} %constant.8.clone.t_fwd, ...), custom_call_target="tpu_custom_call" | custom-call | tf_op jit(solution)/shard_map/afno_tangent/pallas_call | solution.py:412
  183.9 4.5 %copy.11 = f32[45,180,96]{2,1,0:T(8,128)} copy(f32[45,180,96]{2,1,0:T(8,128)} %afno_tangent.1) | data formatting | bytes 6220800

commit v2 on v1

v2 whole, which is shorter than its diff:
```python
import functools
import math

import jax
import jax.numpy as jnp
import ml_dtypes
import numpy as np
from jax import lax
from jax.experimental import pallas as pl
from jax.experimental.pallas import tpu as pltpu
from jax.sharding import PartitionSpec as P

MESH = pl.DeviceIdType.MESH
STEPS = (0, 1, 7, 2, 6, 3, 5, 4)
W = 720
H = 360
C = 96
KW = 256
NB = 8
NX = 4
NS = 32
HL = 45
WL = 180
WP = 184
KP = 192
RP = 12
NG = 3
MP = 384
NT = 9
MSG = NT * 8
MSG2 = 40
F32 = jnp.float32
BF16 = jnp.bfloat16


def split_table(table):
    high = table.astype(ml_dtypes.bfloat16)
    low = (table - high.astype(np.float64)).astype(ml_dtypes.bfloat16)
    return np.stack([high, low])


@functools.lru_cache(None)
def tables():
    depth_z = np.arange(NB)[:, None, None]
    part = np.arange(2)[None, :, None]
    dest = np.arange(NS)[None, None, :]
    mode = 64 * (dest // 8) + 8 * depth_z + dest % 8 + 0 * part
    part = part + 0 * mode
    mode, part = mode.reshape(NB, 64), part.reshape(NB, 64)

    def wave(angle, which):
        return np.where(which == 0, np.cos(angle), -np.sin(angle))

    depth = np.arange(NX * KP)
    lon = 180 * (depth // KP) + depth % KP
    angle = 2 * math.pi / W * (mode[:, :, None] * lon % W)
    forward = wave(angle, part[:, :, None]) / math.sqrt(W) * (depth % KP < WL)

    rows = np.arange(NX * WP)
    lon = 180 * (rows // WP) + rows % WP
    angle = 2 * math.pi / W * (mode[:, None, :] * lon[:, None] % W)
    factor = np.where(mode == 0, 1.0, 2.0)[:, None, :]
    back = wave(angle, part[:, None, :]) * factor / math.sqrt(W) * (rows % WP < WL)[:, None]

    place = np.arange(MP)
    source = place % NS
    local_row = RP * (source // 8) + place // NS
    lat = HL * (source % 8) + local_row
    m = np.arange(MP)
    angle = 2 * math.pi / H * (m[:, None] * lat[None, :] % H)
    keep = (m < H)[:, None] * (local_row < HL)[None, :] / math.sqrt(H)
    cosine, sine = np.cos(angle) * keep, np.sin(angle) * keep
    lat_fwd = np.block([[cosine, sine], [-sine, cosine]])
    lat_back = lat_fwd.T
    order = (np.arange(NB)[:, None] + np.array(STEPS)[None, :]) % NB
    back = back[order].reshape(NB, 4, 2, NX * WP, 64).transpose(0, 1, 3, 2, 4).reshape(NB, 4, NX * WP, 128)
    return tuple(split_table(t) for t in (forward, lat_fwd, lat_back, back))


def high_low(value):
    high = value.astype(BF16)
    return high, (value - high.astype(F32)).astype(BF16)


def dot3(a, b, dims=((1,), (0,))):
    def one(p, q):
        return lax.dot_general(p, q, (dims, ((), ())), preferred_element_type=F32)

    return one(a[0], b[0]) + (one(a[0], b[1]) + one(a[1], b[0]))


NT_DIMS = ((1,), (1,))


def kernel(
    fields, w1, w2, gate, shrink, t_fwd, t_lat, t_bck, t_inv, out,
    fv, xs, xr, xhi, xlo, ys, yr, cs0, cr0, cs1, cr1, osn, gl, sl, gv, sv, wv, wt,
    vfwd, vlat, vbck, vinv, shi, slo, phi, plo, hhi, hlo, mhi, mlo,
    s_load, sf, sa, ra, sb, rb, sc, rc, sd, rd, sm, rm,
):
    x = lax.axis_index("lon")
    t = lax.axis_index("lat")
    z = t // 8
    yc = t % 8
    y = yc // 2
    core = yc % 2
    me = x * 8 + yc

    def field_copies(g):
        copies = []
        for s in range(NX):
            base = RP * s + 4 * g
            rows = pl.ds(base, min(4, HL - base))
            copies.append(pltpu.make_async_copy(fields.at[rows], fv.at[rows], sf.at[g, s]))
        return copies

    stages = [
        pltpu.make_async_copy(gate.at[0], gl, s_load.at[6]),
        pltpu.make_async_copy(shrink.at[0], sl, s_load.at[7]),
    ]
    for copy in stages:
        copy.start()
    for g in range(NG):
        for copy in field_copies(g):
            copy.start()
    loads = [
        pltpu.make_async_copy(w1.at[z], wv.at[0], s_load.at[0]),
        pltpu.make_async_copy(w2.at[z], wv.at[1], s_load.at[1]),
        pltpu.make_async_copy(t_fwd, vfwd, s_load.at[2]),
        pltpu.make_async_copy(t_lat, vlat, s_load.at[3]),
        pltpu.make_async_copy(t_bck, vbck, s_load.at[4]),
        pltpu.make_async_copy(t_inv.at[:, z], vinv, s_load.at[5]),
    ]
    def plane_peer(i):
        dx, r = i % 4, i // 4
        px = (x + dx) % 4
        py = (y + r // 2 + dx) % 4
        pc = (core + r + dx) % 2
        return px * 8 + py * 2 + pc

    def plane_id(d):
        return (d // 8, z * 8 + d % 8)

    barrier = pltpu.get_barrier_semaphore()

    @pl.loop(1, NS)
    def _(i):
        pl.semaphore_signal(barrier, inc=1, device_id=plane_id(plane_peer(i)), device_id_type=MESH)

    @pl.loop(1, NB)
    def _(i):
        pl.semaphore_signal(barrier, inc=1, device_id=(x, ((z + i) % 8) * 8 + yc), device_id_type=MESH)

    def pack(g, dx, put):
        base = RP * ((x + dx) % 4) + 4 * g
        last = fv[base + 3]
        for j in range(3):
            put(j, jnp.concatenate([fv[base + j], last[:, 32 * j : 32 * j + 32]], axis=1))

    def pack_group(g):
        for dx in (2, 1, 3):

            def put(j, value):
                xs[g, dx - 1, j, WP - 8 : WP] = jnp.zeros((8, 128), F32)
                xs[g, dx - 1, j, 0:WL] = value

            pack(g, dx, put)

    def send_group(g):
        for dx in (2, 1, 3):
            pltpu.make_async_remote_copy(
                src_ref=xs.at[g, dx - 1], dst_ref=xr.at[g, x], send_sem=sa.at[g], recv_sem=ra.at[g],
                device_id=((x + dx) % 4, t), device_id_type=MESH,
            ).start()

    def send_mask(src, dst, b, which):
        pltpu.make_async_remote_copy(
            src_ref=src.at[:, b], dst_ref=dst.at[z], send_sem=sm, recv_sem=rm.at[which],
            device_id=(x, b * 8 + yc), device_id_type=MESH,
        ).start()

    for copy in stages:
        copy.wait()
    pl.semaphore_wait(barrier, NS - 1 + NB - 1)
    for step, which in ((1, 0), (7, 0), (2, 0), (6, 1), (3, 1)):
        send_mask(gl, gv, (z + NB - step) % NB, which)
        send_mask(sl, sv, (z + NB - step) % NB, which)
    for src, dst, which in ((gl, gv, 2), (sl, sv, 3)):
        for step in (5, 4):
            send_mask(src, dst, (z + NB - step) % NB, which)
    pltpu.make_async_copy(gate.at[0, :, z], gv.at[z], rm.at[0]).start()
    pltpu.make_async_copy(shrink.at[0, :, z], sv.at[z], rm.at[0]).start()

    for copy in field_copies(0):
        copy.wait()
    pack_group(0)
    send_group(0)
    for copy in loads:
        copy.start()
    fv[HL : RP * NX] = jnp.zeros((RP * NX - HL, WL, C), F32)

    for g in range(1, NG):
        for copy in field_copies(g):
            copy.wait()
        pack_group(g)
        send_group(g)

    for g in range(NG):

        def put(j, value):
            xr[g, x, j, WP - 8 : WP] = jnp.zeros((8, 128), F32)
            xr[g, x, j, 0:WL] = value

        pack(g, 0, put)

    hhi[...] = jnp.zeros_like(hhi)
    hlo[...] = jnp.zeros_like(hlo)
    mhi[...] = jnp.zeros_like(mhi)
    mlo[...] = jnp.zeros_like(mlo)
    cs1[:, :, 36:40, :] = jnp.zeros((2, NS, 4, 128), F32)

    for copy in loads:
        copy.wait()
    for which in range(2):
        wt[...] = jnp.zeros((256, 256), F32)
        wt[0:C, 0:C] = wv[which, 0]
        wt[0:C, 128 : 128 + C] = wv[which, 1]
        wt[128 : 128 + C, 0:C] = -wv[which, 1]
        wt[128 : 128 + C, 128 : 128 + C] = wv[which, 0]
        turned = wt[...].T
        high, low = high_low(turned)
        if which == 0:
            w1t = (high, low)
        else:
            w2t = (high, low)

    def mode_at(u):
        return (z + STEPS[u]) % NB

    ysflat = ys.reshape(2, NS * MSG, 128)
    for g in range(NG):
        pltpu.make_async_copy(xr.at[g, pl.ds(0, 3)], xr.at[g, pl.ds(0, 3)], ra.at[g]).wait()
        for s in range(NX):
            for j in range(3):
                value = jnp.concatenate([xr[g, s, j], jnp.zeros((KP - WP, 128), F32)], axis=0)
                high, low = high_low(value)
                xhi[KP * s : KP * s + KP, 128 * j : 128 * j + 128] = high
                xlo[KP * s : KP * s + KP, 128 * j : 128 * j + 128] = low
        for half in range(2):
            table = [jnp.concatenate([vfwd[k, mode_at(4 * half + u)] for u in range(4)], axis=0) for k in range(2)]
            modes = dot3(table, (xhi[...], xlo[...]))
            for u in range(4):
                for ri in range(2):
                    for j in range(3):
                        start = (3 * g + j) * 8 + ri * 4 + u
                        ysflat[half, pl.ds(start, NS, stride=MSG), :] = modes[
                            64 * u + 32 * ri : 64 * u + 32 * ri + 32, 128 * j : 128 * j + 128
                        ]
            if g == NG - 1:
                own = pltpu.make_async_copy(ys.at[half, me], yr.at[half, me], rb.at[half])
                own.start()

                @pl.loop(1, NS)
                def _(i):
                    d = plane_peer(i)
                    pltpu.make_async_remote_copy(
                        src_ref=ys.at[half, d], dst_ref=yr.at[half, me], send_sem=sb.at[half], recv_sem=rb.at[half],
                        device_id=plane_id(d), device_id_type=MESH,
                    ).start()

    yflat = yr.reshape(2, NS * MSG, 128)
    cs0flat = cs0.reshape(NS * MSG, 128)
    cs1flat = cs1.reshape(2, NS * MSG2, 128)
    cr0flat = cr0.reshape(NS * MSG, 128)
    cr1flat = cr1.reshape(2, NS * MSG2, 128)

    def lat_forward(half, slot):
        for pos in range(2):
            for ri in range(2):
                for g in range(NG):
                    tiles = [
                        yflat[half, pl.ds((3 * g + j) * 8 + ri * 4 + 2 * slot + pos, NS, stride=MSG), :]
                        for j in range(3)
                    ]
                    last = jnp.concatenate([v[:, C:] for v in tiles] + [tiles[0][:, C:]], axis=1)
                    for r, value in enumerate(tiles + [last]):
                        high, low = high_low(value)
                        at = ri * MP + (g * 4 + r) * NS
                        shi[at : at + NS, 128 * pos : 128 * pos + 128] = high
                        slo[at : at + NS, 128 * pos : 128 * pos + 128] = low
        spec = dot3((vlat[0], vlat[1]), (shi[...], slo[...]))
        for pos in range(2):
            for ri in range(2):
                high, low = high_low(spec[MP * ri : MP * ri + MP, 128 * pos : 128 * pos + 128])
                phi[pos, :, 128 * ri : 128 * ri + 128] = high
                plo[pos, :, 128 * ri : 128 * ri + 128] = low

    def lat_back(modes, put, ready=None):
        for pos, q in enumerate(modes):
            hid = dot3(w1t, (phi[pos], plo[pos]), NT_DIMS)
            for ri in range(2):
                high, low = high_low(hid[128 * ri : 128 * ri + C, 0:H] * gv[q, ri].astype(F32))
                hhi[128 * ri : 128 * ri + C, 0:H] = high
                hlo[128 * ri : 128 * ri + C, 0:H] = low
            mix = dot3(w2t, (hhi[...], hlo[...]))
            if ready is not None and pos == 0:
                ready()
            for ri in range(2):
                high, low = high_low(mix[128 * ri : 128 * ri + C, 0:H] * sv[q, ri].astype(F32))
                mhi[128 * pos : 128 * pos + C, MP * ri : MP * ri + H] = high
                mlo[128 * pos : 128 * pos + C, MP * ri : MP * ri + H] = low
        band = dot3((vbck[0], vbck[1]), (mhi[...], mlo[...]), NT_DIMS)
        for pos in range(2):
            for ri in range(2):
                for g in range(NG):
                    at = ri * MP + g * 4 * NS
                    rows = [band[at + r * NS : at + r * NS + NS, 128 * pos : 128 * pos + 128] for r in range(4)]
                    for j in range(3):
                        value = jnp.concatenate([rows[j][:, 0:C], rows[3][:, 32 * j : 32 * j + 32]], axis=1)
                        put(3 * g + j, ri, pos, value)

    def send_back(src, dst, which):
        pltpu.make_async_copy(src.at[me], dst.at[me], rc.at[which]).start()

        @pl.loop(1, NS)
        def _(i):
            d = plane_peer(i)
            pltpu.make_async_remote_copy(
                src_ref=src.at[d], dst_ref=dst.at[me], send_sem=sc.at[which], recv_sem=rc.at[which],
                device_id=plane_id(d), device_id_type=MESH,
            ).start()

    def lat_single(i, ready=None):
        slot = i - 2

        def put(tile, ri, pos, value):
            cs1flat[slot, pl.ds(tile * 4 + ri * 2 + pos, NS, stride=MSG2), :] = value

        lat_back((mode_at(2 * i), mode_at(2 * i + 1)), put, ready)
        send_back(cs1.at[slot], cr1.at[slot], 1 + slot)

    def inverse_term(g, units, rows, pairs):
        for u in range(units):
            for ri in range(2):
                for j in range(3):
                    high, low = high_low(rows(3 * g + j, ri, u))
                    at = 64 * u + 32 * ri
                    xhi[at : at + 32, 128 * j : 128 * j + 128] = high
                    xlo[at : at + 32, 128 * j : 128 * j + 128] = low
        table = [jnp.concatenate([vinv[k, i] for i in pairs], axis=1) for k in range(2)]
        return dot3(table, (xhi[0 : 64 * units], xlo[0 : 64 * units]))

    def rows_first(tile, ri, u):
        return cr0flat[pl.ds(tile * 8 + ri * 4 + u, NS, stride=MSG), :]

    def rows_single(slot):
        return lambda tile, ri, u: cr1flat[slot, pl.ds(tile * 4 + ri * 2 + u, NS, stride=MSG2), :]

    pltpu.make_async_copy(yr.at[0], yr.at[0], rb.at[0]).wait()
    pltpu.make_async_copy(gv, gv, rm.at[0]).wait()

    @pl.loop(0, 2)
    def _(slot):
        def put(tile, ri, pos, value):
            cs0flat[pl.ds(tile * 8 + ri * 4 + 2 * slot + pos, NS, stride=MSG), :] = value

        lat_forward(0, slot)
        lat_back(((z + 7 * slot) % NB, (z + 1 + slot) % NB), put)

    send_back(cs0, cr0, 0)

    pltpu.make_async_copy(yr.at[1], yr.at[1], rb.at[1]).wait()
    pltpu.make_async_copy(gv.at[pl.ds(0, 4)], gv.at[pl.ds(0, 4)], rm.at[1]).wait()
    lat_forward(1, 0)
    lat_single(2)
    lat_forward(1, 1)

    pltpu.make_async_copy(cr0, cr0, rc.at[0]).wait()
    for g in range(NG):
        term = inverse_term(g, 4, rows_first, (0, 1))
        for s in range(NX):
            for j in range(3):
                osn[g, s, j] = term[WP * s : WP * s + WP, 128 * j : 128 * j + 128]

    def add_single(slot, g):
        term = inverse_term(g, 2, rows_single(slot), (2 + slot,))
        for s in range(NX):
            for j in range(3):
                osn[g, s, j] += term[WP * s : WP * s + WP, 128 * j : 128 * j + 128]

    pltpu.make_async_copy(cr1.at[0], cr1.at[0], rc.at[1]).wait()
    for g in range(NG):
        add_single(0, g)

    pltpu.make_async_copy(gv.at[pl.ds(0, 2)], gv.at[pl.ds(0, 2)], rm.at[2]).wait()
    lat_single(3, lambda: pltpu.make_async_copy(sv.at[pl.ds(0, 2)], sv.at[pl.ds(0, 2)], rm.at[3]).wait())

    pltpu.make_async_copy(cr1.at[1], cr1.at[1], rc.at[2]).wait()
    for g in range(NG):
        add_single(1, g)
        pltpu.make_async_copy(osn.at[g, x], out.at[g, x], rd.at[g]).start()
        for dx in (2, 1, 3):
            to = (x + dx) % 4
            pltpu.make_async_remote_copy(
                src_ref=osn.at[g, to], dst_ref=out.at[g, x], send_sem=sd.at[g], recv_sem=rd.at[g],
                device_id=(to, t), device_id_type=MESH,
            ).start()

    for g in range(NG):
        pltpu.make_async_copy(osn.at[g], osn.at[g], rd.at[g]).wait()
    for g in range(NG):
        pltpu.make_async_copy(xs.at[g], xs.at[g], sa.at[g]).wait()
        pltpu.make_async_copy(xs.at[g], xs.at[g], sd.at[g]).wait()
    for half in range(2):
        sent = ys.at[half, pl.ds(0, NS - 1)]
        pltpu.make_async_copy(sent, sent, sb.at[half]).wait()
        sent = cs1.at[half, pl.ds(0, NS - 1)]
        pltpu.make_async_copy(sent, sent, sc.at[1 + half]).wait()
    sent = cs0.at[pl.ds(0, NS - 1)]
    pltpu.make_async_copy(sent, sent, sc.at[0]).wait()
    pltpu.make_async_copy(gv.at[pl.ds(0, 7)], gv.at[pl.ds(0, 7)], sm).wait()
    pltpu.make_async_copy(gv.at[pl.ds(0, 7)], gv.at[pl.ds(0, 7)], sm).wait()


def unpack(packed, out, tiles, rows, s_in, s_out):
    def load(g, s):
        return pltpu.make_async_copy(packed.at[g, s], tiles.at[g, s], s_in.at[g, s])

    def store(g, s):
        base = RP * s + 4 * g
        span = pl.ds(base, min(4, HL - base))
        return pltpu.make_async_copy(rows.at[span], out.at[span], s_out.at[g, s])

    order = [(g, s) for s in range(NX) for g in range(NG)]
    for g, s in order:
        load(g, s).start()
    for g, s in order:
        load(g, s).wait()
        base = RP * s + 4 * g
        count = min(4, HL - base)
        for r in range(min(3, count)):
            rows[base + r] = tiles[g, s, r, 0:WL, 0:C]
        if count == 4:
            rows[base + 3] = jnp.concatenate([tiles[g, s, r, 0:WL, C:] for r in range(3)], axis=1)
        store(g, s).start()
    for g, s in order:
        store(g, s).wait()


def local(fields, weight_one, weight_two, gate_mask, shrink_mask):
    gate = jnp.swapaxes(gate_mask, 3, 4)
    shrink = jnp.swapaxes(shrink_mask, 3, 4)
    consts = [jnp.asarray(t) for t in tables()]
    dma = pltpu.SemaphoreType.DMA
    any_spec = pl.BlockSpec(memory_space=pl.ANY)
    vm = pltpu.VMEM
    scratch = [
        vm((RP * NX, WL, C), F32),
        vm((NG, 3, 3, WP, 128), F32),
        vm((NG, NX, 3, WP, 128), F32),
        vm((NX * KP, 384), BF16),
        vm((NX * KP, 384), BF16),
        vm((2, NS, MSG, 128), F32),
        vm((2, NS, MSG, 128), F32),
        vm((NS, MSG, 128), F32),
        vm((NS, MSG, 128), F32),
        vm((2, NS, MSG2, 128), F32),
        vm((2, NS, MSG2, 128), F32),
        vm((NG, NX, 3, WP, 128), F32),
        vm((2, NB, C, H), jnp.int32),
        vm((2, NB, C, H), jnp.int32),
        vm((NB, 2, C, H), jnp.int32),
        vm((NB, 2, C, H), jnp.int32),
        vm((2, 2, C, C), F32),
        vm((256, 256), F32),
        vm((2, NB, 64, NX * KP), BF16),
        vm((2, 2 * MP, 2 * MP), BF16),
        vm((2, 2 * MP, 2 * MP), BF16),
        vm((2, 4, NX * WP, 128), BF16),
        vm((2 * MP, 256), BF16),
        vm((2 * MP, 256), BF16),
        vm((2, MP, 256), BF16),
        vm((2, MP, 256), BF16),
        vm((256, MP), BF16),
        vm((256, MP), BF16),
        vm((256, 2 * MP), BF16),
        vm((256, 2 * MP), BF16),
        dma((8,)),
        dma((NG, NX)),
        dma((NG,)),
        dma((NG,)),
        dma((2,)),
        dma((2,)),
        dma((3,)),
        dma((3,)),
        dma((NG,)),
        dma((NG,)),
        dma,
        dma((4,)),
    ]
    packed = pl.pallas_call(
        kernel,
        name="afno_tangent",
        out_shape=jax.ShapeDtypeStruct((NG, NX, 3, WP, 128), F32),
        in_specs=[any_spec] * 9,
        out_specs=any_spec,
        scratch_shapes=scratch,
        compiler_params=pltpu.CompilerParams(
            collective_id=0, has_side_effects=True, vmem_limit_bytes=62 * 2**20
        ),
    )(fields, weight_one, weight_two, gate, shrink, *consts)
    return pl.pallas_call(
        unpack,
        name="unpack_rows",
        out_shape=jax.ShapeDtypeStruct((HL, WL, C), F32),
        in_specs=[any_spec],
        out_specs=any_spec,
        scratch_shapes=[vm((NG, NX, 3, WP, 128), F32), vm((HL, WL, C), F32), dma((NG, NX)), dma((NG, NX))],
        compiler_params=pltpu.CompilerParams(vmem_limit_bytes=60 * 2**20),
    )(packed)


def solution(mesh):
    in_specs = (
        P("lat", "lon", None),
        P(),
        P(),
        P(("lon", "lat"), None, None, None, None),
        P(("lon", "lat"), None, None, None, None),
    )
    out_specs = P("lat", "lon", None)
    return jax.shard_map(local, mesh=mesh, in_specs=in_specs, out_specs=out_specs, check_vma=False)
```

time: 189 us -> 172 us (0.910)
  Pallas kernels: 184 us -> 172 us
  local copies, waits for them, and re-layouts: 4.5 us -> 0 us
    pallas_call x1, Pallas kernels: 184 us -> 168 us  [local(): pl.pallas_call(kernel, name='afno_tangent', out_shape=jax.ShapeDtypeStruc...]
    unnamed x1 -> x0, local copies, waits for them, and re-layouts: 4.5 us -> none
    pallas_call x0 -> x1, Pallas kernels: none -> 3.49 us  [local(): pl.pallas_call(unpack, name='unpack_rows', out_shape=jax.ShapeDtypeStruct...]
where the time goes in v2:
time: 172 us
  Pallas kernels  172 us (100%)
    pallas_call x1, Pallas kernels, local(): pl.pallas_call(kernel, name='afno_tangent', out_shape=jax.ShapeDtypeStruc...  168 us
    pallas_call x1, Pallas kernels, local(): pl.pallas_call(unpack, name='unpack_rows', out_shape=jax.ShapeDtypeStruct...  3.49 us

profile of v2, /device:TPU:1, one launch (start us, length us, event | category | flops | bytes accessed | tf_op | source)
XLA Modules:
  0.0 171.7 jit_solution(18096001322541244690)
XLA Ops:
  0.0 168.1 %afno_tangent.1.packed = f32[3,4,3,184,128]{4,3,2,1,0:T(8,128)} custom-call(f32[45,180,96]{2,1,0:T(8,128)} %fields.1, f32[8,2,96,96]{3,2,1,0:T(8,128)} %w1.1, f32[8,2,96,96]{3,2,1,0:T(8,128)} %w2.1, s32[1,2,8,96,360]{4,3,2,1,0:T(8,128)} %bitcast.2, s32[1,2,8,96,360]{4,3,2,1,0:T(8,128)} %bitcast.3, bf16[2,8,64,768]{3,2,1,0:T(8,128)(2,1)} %constant.8.clone.t_fwd, ...), custom_call_target="tpu_custom_call" | custom-call | tf_op jit(solution)/shard_map/afno_tangent/pallas_call | solution.py:501
  168.1 3.5 %unpack_rows.1 = f32[45,180,96]{2,1,0:T(8,128)} custom-call(f32[3,4,3,184,128]{4,3,2,1,0:T(8,128)} %afno_tangent.1.packed), custom_call_target="tpu_custom_call" | custom-call | tf_op jit(solution)/shard_map/unpack_rows/pallas_call | solution.py:512

commit v3 on v2

--- a/solution.py
+++ b/solution.py
@@ -29,6 +29,7 @@
 NT = 9
 MSG = NT * 8
 MSG2 = 40
+MSG1 = 24
 F32 = jnp.float32
 BF16 = jnp.bfloat16
 
@@ -94,7 +95,8 @@
 
 def kernel(
     fields, w1, w2, gate, shrink, t_fwd, t_lat, t_bck, t_inv, out,
-    fv, xs, xr, xhi, xlo, ys, yr, cs0, cr0, cs1, cr1, osn, gl, sl, gv, sv, wv, wt,
+    fv, xs, xr, xhi, xlo, ys0, yr0, ys1, yr1,
+    cs0, cr0, cs1, cr1, cs2, cr2, cs3, cr3, osn, gl, sl, gv, sv, wv, wt,
     vfwd, vlat, vbck, vinv, shi, slo, phi, plo, hhi, hlo, mhi, mlo,
     s_load, sf, sa, ra, sb, rb, sc, rc, sd, rd, sm, rm,
 ):
@@ -114,13 +116,15 @@
             copies.append(pltpu.make_async_copy(fields.at[rows], fv.at[rows], sf.at[g, s]))
         return copies
 
+    for copy in field_copies(0):
+        copy.start()
     stages = [
         pltpu.make_async_copy(gate.at[0], gl, s_load.at[6]),
         pltpu.make_async_copy(shrink.at[0], sl, s_load.at[7]),
     ]
     for copy in stages:
         copy.start()
-    for g in range(NG):
+    for g in range(1, NG):
         for copy in field_copies(g):
             copy.start()
     loads = [
@@ -132,20 +136,21 @@
         pltpu.make_async_copy(t_inv.at[:, z], vinv, s_load.at[5]),
     ]
     def plane_peer(i):
-        dx, r = i % 4, i // 4
-        px = (x + dx) % 4
-        py = (y + r // 2 + dx) % 4
-        pc = (core + r + dx) % 2
+        dx, r = lax.rem(i, 4), lax.div(i, 4)
+        px = lax.rem(x + dx, 4)
+        py = lax.rem(y + lax.div(r, 2) + dx, 4)
+        pc = lax.rem(core + r + dx, 2)
         return px * 8 + py * 2 + pc
 
     def plane_id(d):
-        return (d // 8, z * 8 + d % 8)
+        return (lax.div(d, 8), z * 8 + lax.rem(d, 8))
 
     barrier = pltpu.get_barrier_semaphore()
 
     @pl.loop(1, NS)
     def _(i):
-        pl.semaphore_signal(barrier, inc=1, device_id=plane_id(plane_peer(i)), device_id_type=MESH)
+        d = plane_peer(i)
+        pl.semaphore_signal(barrier, inc=1, device_id=plane_id(d), device_id_type=MESH)
 
     @pl.loop(1, NB)
     def _(i):
@@ -179,22 +184,22 @@
             device_id=(x, b * 8 + yc), device_id_type=MESH,
         ).start()
 
+    for copy in field_copies(0):
+        copy.wait()
+    pack_group(0)
     for copy in stages:
         copy.wait()
     pl.semaphore_wait(barrier, NS - 1 + NB - 1)
     for step, which in ((1, 0), (7, 0), (2, 0), (6, 1), (3, 1)):
         send_mask(gl, gv, (z + NB - step) % NB, which)
         send_mask(sl, sv, (z + NB - step) % NB, which)
-    for src, dst, which in ((gl, gv, 2), (sl, sv, 3)):
-        for step in (5, 4):
-            send_mask(src, dst, (z + NB - step) % NB, which)
+    for step, which in ((5, 2), (4, 3)):
+        send_mask(gl, gv, (z + NB - step) % NB, which)
+        send_mask(sl, sv, (z + NB - step) % NB, which)
+    send_group(0)
     pltpu.make_async_copy(gate.at[0, :, z], gv.at[z], rm.at[0]).start()
     pltpu.make_async_copy(shrink.at[0, :, z], sv.at[z], rm.at[0]).start()
 
-    for copy in field_copies(0):
-        copy.wait()
-    pack_group(0)
-    send_group(0)
     for copy in loads:
         copy.start()
     fv[HL : RP * NX] = jnp.zeros((RP * NX - HL, WL, C), F32)
@@ -217,27 +222,38 @@
     hlo[...] = jnp.zeros_like(hlo)
     mhi[...] = jnp.zeros_like(mhi)
     mlo[...] = jnp.zeros_like(mlo)
-    cs1[:, :, 36:40, :] = jnp.zeros((2, NS, 4, 128), F32)
+    cs1[:, 36:MSG2, :] = jnp.zeros((NS, MSG2 - 36, 128), F32)
+    for ref in (cs2, cs3):
+        ref[:, 18:MSG1, :] = jnp.zeros((NS, MSG1 - 18, 128), F32)
 
     for copy in loads:
         copy.wait()
+    turned_weights = []
     for which in range(2):
         wt[...] = jnp.zeros((256, 256), F32)
         wt[0:C, 0:C] = wv[which, 0]
         wt[0:C, 128 : 128 + C] = wv[which, 1]
         wt[128 : 128 + C, 0:C] = -wv[which, 1]
         wt[128 : 128 + C, 128 : 128 + C] = wv[which, 0]
-        turned = wt[...].T
-        high, low = high_low(turned)
-        if which == 0:
-            w1t = (high, low)
-        else:
-            w2t = (high, low)
+        turned_weights.append(high_low(wt[...].T))
 
     def mode_at(u):
         return (z + STEPS[u]) % NB
 
-    ysflat = ys.reshape(2, NS * MSG, 128)
+    def send_plane(src, dst, send_sem, recv_sem, which):
+        pltpu.make_async_copy(src.at[me], dst.at[me], recv_sem.at[which]).start()
+
+        @pl.loop(1, NS)
+        def _(i):
+            d = plane_peer(i)
+            pltpu.make_async_remote_copy(
+                src_ref=src.at[d], dst_ref=dst.at[me], send_sem=send_sem.at[which], recv_sem=recv_sem.at[which],
+                device_id=plane_id(d), device_id_type=MESH,
+            ).start()
+
+    ys0flat = ys0.reshape(NS * MSG, 128)
+    ys1flat = ys1.reshape(NS * MSG, 128)
+    ysflat = (ys0flat, ys1flat)
     for g in range(NG):
         pltpu.make_async_copy(xr.at[g, pl.ds(0, 3)], xr.at[g, pl.ds(0, 3)], ra.at[g]).wait()
         for s in range(NX):
@@ -252,36 +268,33 @@
             for u in range(4):
                 for ri in range(2):
                     for j in range(3):
-                        start = (3 * g + j) * 8 + ri * 4 + u
-                        ysflat[half, pl.ds(start, NS, stride=MSG), :] = modes[
-                            64 * u + 32 * ri : 64 * u + 32 * ri + 32, 128 * j : 128 * j + 128
-                        ]
-            if g == NG - 1:
-                own = pltpu.make_async_copy(ys.at[half, me], yr.at[half, me], rb.at[half])
-                own.start()
-
-                @pl.loop(1, NS)
-                def _(i):
-                    d = plane_peer(i)
-                    pltpu.make_async_remote_copy(
-                        src_ref=ys.at[half, d], dst_ref=yr.at[half, me], send_sem=sb.at[half], recv_sem=rb.at[half],
-                        device_id=plane_id(d), device_id_type=MESH,
-                    ).start()
-
-    yflat = yr.reshape(2, NS * MSG, 128)
+                        value = modes[64 * u + 32 * ri : 64 * u + 32 * ri + 32, 128 * j : 128 * j + 128]
+                        row = 2 * (3 * g + j) + ri
+                        ysflat[half][pl.ds(4 * row + u, NS, stride=MSG), :] = value
+            if g == NG - 1 and half == 0:
+                send_plane(ys0, yr0, sb, rb, 0)
+            elif g == NG - 1:
+                send_plane(ys1, yr1, sb, rb, 1)
+
+    yr0flat = yr0.reshape(NS * MSG, 128)
+    yr1flat = yr1.reshape(NS * MSG, 128)
     cs0flat = cs0.reshape(NS * MSG, 128)
-    cs1flat = cs1.reshape(2, NS * MSG2, 128)
+    cs1flat = cs1.reshape(NS * MSG2, 128)
+    cs2flat = cs2.reshape(NS * MSG1, 128)
+    cs3flat = cs3.reshape(NS * MSG1, 128)
     cr0flat = cr0.reshape(NS * MSG, 128)
-    cr1flat = cr1.reshape(2, NS * MSG2, 128)
-
-    def lat_forward(half, slot):
-        for pos in range(2):
+    cr1flat = cr1.reshape(NS * MSG2, 128)
+    cr2flat = cr2.reshape(NS * MSG1, 128)
+    cr3flat = cr3.reshape(NS * MSG1, 128)
+
+    def strided(ref, units, pitch, unit):
+        return lambda row: ref[pl.ds(units * row + unit, NS, stride=pitch), :]
+
+    def lat_forward(sources):
+        for pos, source in enumerate(sources):
             for ri in range(2):
                 for g in range(NG):
-                    tiles = [
-                        yflat[half, pl.ds((3 * g + j) * 8 + ri * 4 + 2 * slot + pos, NS, stride=MSG), :]
-                        for j in range(3)
-                    ]
+                    tiles = [source(2 * (3 * g + j) + ri) for j in range(3)]
                     last = jnp.concatenate([v[:, C:] for v in tiles] + [tiles[0][:, C:]], axis=1)
                     for r, value in enumerate(tiles + [last]):
                         high, low = high_low(value)
@@ -295,109 +308,99 @@
                 phi[pos, :, 128 * ri : 128 * ri + 128] = high
                 plo[pos, :, 128 * ri : 128 * ri + 128] = low
 
-    def lat_back(modes, put, ready=None):
-        for pos, q in enumerate(modes):
-            hid = dot3(w1t, (phi[pos], plo[pos]), NT_DIMS)
+    def lat_back(places, modes, put):
+        first, second = turned_weights
+        for pos, (place, q) in enumerate(zip(places, modes)):
+            hid = dot3(first, (phi[place], plo[place]), NT_DIMS)
             for ri in range(2):
                 high, low = high_low(hid[128 * ri : 128 * ri + C, 0:H] * gv[q, ri].astype(F32))
                 hhi[128 * ri : 128 * ri + C, 0:H] = high
                 hlo[128 * ri : 128 * ri + C, 0:H] = low
-            mix = dot3(w2t, (hhi[...], hlo[...]))
-            if ready is not None and pos == 0:
-                ready()
+            mix = dot3(second, (hhi[...], hlo[...]))
             for ri in range(2):
                 high, low = high_low(mix[128 * ri : 128 * ri + C, 0:H] * sv[q, ri].astype(F32))
                 mhi[128 * pos : 128 * pos + C, MP * ri : MP * ri + H] = high
                 mlo[128 * pos : 128 * pos + C, MP * ri : MP * ri + H] = low
-        band = dot3((vbck[0], vbck[1]), (mhi[...], mlo[...]), NT_DIMS)
-        for pos in range(2):
+        width = 128 * len(modes)
+        band = dot3((vbck[0], vbck[1]), (mhi[0:width], mlo[0:width]), NT_DIMS)
+        for pos in range(len(modes)):
             for ri in range(2):
                 for g in range(NG):
                     at = ri * MP + g * 4 * NS
                     rows = [band[at + r * NS : at + r * NS + NS, 128 * pos : 128 * pos + 128] for r in range(4)]
                     for j in range(3):
                         value = jnp.concatenate([rows[j][:, 0:C], rows[3][:, 32 * j : 32 * j + 32]], axis=1)
-                        put(3 * g + j, ri, pos, value)
-
-    def send_back(src, dst, which):
-        pltpu.make_async_copy(src.at[me], dst.at[me], rc.at[which]).start()
-
-        @pl.loop(1, NS)
-        def _(i):
-            d = plane_peer(i)
-            pltpu.make_async_remote_copy(
-                src_ref=src.at[d], dst_ref=dst.at[me], send_sem=sc.at[which], recv_sem=rc.at[which],
-                device_id=plane_id(d), device_id_type=MESH,
-            ).start()
-
-    def lat_single(i, ready=None):
-        slot = i - 2
-
-        def put(tile, ri, pos, value):
-            cs1flat[slot, pl.ds(tile * 4 + ri * 2 + pos, NS, stride=MSG2), :] = value
-
-        lat_back((mode_at(2 * i), mode_at(2 * i + 1)), put, ready)
-        send_back(cs1.at[slot], cr1.at[slot], 1 + slot)
-
-    def inverse_term(g, units, rows, pairs):
-        for u in range(units):
+                        put(2 * (3 * g + j) + ri, pos, value)
+
+    def inverse_term(g, sources, slots):
+        for u, source in enumerate(sources):
             for ri in range(2):
                 for j in range(3):
-                    high, low = high_low(rows(3 * g + j, ri, u))
+                    high, low = high_low(source(2 * (3 * g + j) + ri))
                     at = 64 * u + 32 * ri
                     xhi[at : at + 32, 128 * j : 128 * j + 128] = high
                     xlo[at : at + 32, 128 * j : 128 * j + 128] = low
-        table = [jnp.concatenate([vinv[k, i] for i in pairs], axis=1) for k in range(2)]
-        return dot3(table, (xhi[0 : 64 * units], xlo[0 : 64 * units]))
-
-    def rows_first(tile, ri, u):
-        return cr0flat[pl.ds(tile * 8 + ri * 4 + u, NS, stride=MSG), :]
-
-    def rows_single(slot):
-        return lambda tile, ri, u: cr1flat[slot, pl.ds(tile * 4 + ri * 2 + u, NS, stride=MSG2), :]
-
-    pltpu.make_async_copy(yr.at[0], yr.at[0], rb.at[0]).wait()
-    pltpu.make_async_copy(gv, gv, rm.at[0]).wait()
+        table = [jnp.concatenate([vinv[k, i] for i in slots], axis=1) for k in range(2)]
+        depth = 64 * len(sources)
+        return dot3(table, (xhi[0:depth], xlo[0:depth]))
+
+    def add_term(g, sources, slots, first=False):
+        term = inverse_term(g, sources, slots)
+        for s in range(NX):
+            for j in range(3):
+                value = term[WP * s : WP * s + WP, 128 * j : 128 * j + 128]
+                osn[g, s, j] = value if first else osn[g, s, j] + value
+
+    def arrived(ref, sem):
+        pltpu.make_async_copy(ref, ref, sem).wait()
+
+    arrived(yr0, rb.at[0])
+    arrived(gv, rm.at[0])
 
     @pl.loop(0, 2)
     def _(slot):
-        def put(tile, ri, pos, value):
-            cs0flat[pl.ds(tile * 8 + ri * 4 + 2 * slot + pos, NS, stride=MSG), :] = value
-
-        lat_forward(0, slot)
-        lat_back(((z + 7 * slot) % NB, (z + 1 + slot) % NB), put)
-
-    send_back(cs0, cr0, 0)
-
-    pltpu.make_async_copy(yr.at[1], yr.at[1], rb.at[1]).wait()
-    pltpu.make_async_copy(gv.at[pl.ds(0, 4)], gv.at[pl.ds(0, 4)], rm.at[1]).wait()
-    lat_forward(1, 0)
-    lat_single(2)
-    lat_forward(1, 1)
-
-    pltpu.make_async_copy(cr0, cr0, rc.at[0]).wait()
-    for g in range(NG):
-        term = inverse_term(g, 4, rows_first, (0, 1))
-        for s in range(NX):
-            for j in range(3):
-                osn[g, s, j] = term[WP * s : WP * s + WP, 128 * j : 128 * j + 128]
-
-    def add_single(slot, g):
-        term = inverse_term(g, 2, rows_single(slot), (2 + slot,))
-        for s in range(NX):
-            for j in range(3):
-                osn[g, s, j] += term[WP * s : WP * s + WP, 128 * j : 128 * j + 128]
-
-    pltpu.make_async_copy(cr1.at[0], cr1.at[0], rc.at[1]).wait()
-    for g in range(NG):
-        add_single(0, g)
-
-    pltpu.make_async_copy(gv.at[pl.ds(0, 2)], gv.at[pl.ds(0, 2)], rm.at[2]).wait()
-    lat_single(3, lambda: pltpu.make_async_copy(sv.at[pl.ds(0, 2)], sv.at[pl.ds(0, 2)], rm.at[3]).wait())
-
-    pltpu.make_async_copy(cr1.at[1], cr1.at[1], rc.at[2]).wait()
-    for g in range(NG):
-        add_single(1, g)
+        def put(row, pos, value):
+            cs0flat[pl.ds(4 * row + 2 * slot + pos, NS, stride=MSG), :] = value
+
+        lat_forward([strided(yr0flat, 4, MSG, 2 * slot + pos) for pos in range(2)])
+        lat_back((0, 1), ((z + 7 * slot) % NB, (z + 1 + slot) % NB), put)
+
+    send_plane(cs0, cr0, sc, rc, 0)
+
+    arrived(yr1, rb.at[1])
+    lat_forward([strided(yr1flat, 4, MSG, pos) for pos in range(2)])
+    arrived(gv.at[pl.ds(0, 4)], rm.at[1])
+
+    def put_next(row, pos, value):
+        cs1flat[pl.ds(2 * row + pos, NS, stride=MSG2), :] = value
+
+    lat_back((0, 1), (mode_at(4), mode_at(5)), put_next)
+    send_plane(cs1, cr1, sc, rc, 1)
+
+    lat_forward([strided(yr1flat, 4, MSG, 2 + pos) for pos in range(2)])
+    arrived(cr0, rc.at[0])
+    for g in range(NG):
+        add_term(g, [strided(cr0flat, 4, MSG, u) for u in range(4)], (0, 1), first=True)
+
+    def put_third(row, pos, value):
+        cs2flat[pl.ds(row, NS, stride=MSG1), :] = value
+
+    def put_last(row, pos, value):
+        cs3flat[pl.ds(row, NS, stride=MSG1), :] = value
+
+    arrived(gv.at[pl.ds(0, 2)], rm.at[2])
+    lat_back((0,), (mode_at(6),), put_third)
+    send_plane(cs2, cr2, sc, rc, 2)
+    arrived(cr1, rc.at[1])
+    for g in range(NG):
+        add_term(g, [strided(cr1flat, 2, MSG2, u) for u in range(2)], (2,))
+    arrived(gv.at[pl.ds(0, 2)], rm.at[3])
+    lat_back((1,), (mode_at(7),), put_last)
+    send_plane(cs3, cr3, sc, rc, 3)
+    arrived(cr2, rc.at[2])
+    arrived(cr3, rc.at[3])
+    for g in range(NG):
+        add_term(g, [strided(cr2flat, 1, MSG1, 0), strided(cr3flat, 1, MSG1, 0)], (3,))
         pltpu.make_async_copy(osn.at[g, x], out.at[g, x], rd.at[g]).start()
         for dx in (2, 1, 3):
             to = (x + dx) % 4
@@ -411,15 +414,10 @@
     for g in range(NG):
         pltpu.make_async_copy(xs.at[g], xs.at[g], sa.at[g]).wait()
         pltpu.make_async_copy(xs.at[g], xs.at[g], sd.at[g]).wait()
-    for half in range(2):
-        sent = ys.at[half, pl.ds(0, NS - 1)]
-        pltpu.make_async_copy(sent, sent, sb.at[half]).wait()
-        sent = cs1.at[half, pl.ds(0, NS - 1)]
-        pltpu.make_async_copy(sent, sent, sc.at[1 + half]).wait()
-    sent = cs0.at[pl.ds(0, NS - 1)]
-    pltpu.make_async_copy(sent, sent, sc.at[0]).wait()
-    pltpu.make_async_copy(gv.at[pl.ds(0, 7)], gv.at[pl.ds(0, 7)], sm).wait()
-    pltpu.make_async_copy(gv.at[pl.ds(0, 7)], gv.at[pl.ds(0, 7)], sm).wait()
+    for ref, sem in ((ys0, sb.at[0]), (ys1, sb.at[1]), (cs0, sc.at[0]), (cs1, sc.at[1]), (cs2, sc.at[2]), (cs3, sc.at[3])):
+        arrived(ref.at[pl.ds(0, NS - 1)], sem)
+    arrived(gv.at[pl.ds(0, 7)], sm)
+    arrived(gv.at[pl.ds(0, 7)], sm)
 
 
 def unpack(packed, out, tiles, rows, s_in, s_out):
@@ -460,12 +458,18 @@
         vm((NG, NX, 3, WP, 128), F32),
         vm((NX * KP, 384), BF16),
         vm((NX * KP, 384), BF16),
-        vm((2, NS, MSG, 128), F32),
-        vm((2, NS, MSG, 128), F32),
         vm((NS, MSG, 128), F32),
         vm((NS, MSG, 128), F32),
-        vm((2, NS, MSG2, 128), F32),
-        vm((2, NS, MSG2, 128), F32),
+        vm((NS, MSG, 128), F32),
+        vm((NS, MSG, 128), F32),
+        vm((NS, MSG, 128), F32),
+        vm((NS, MSG, 128), F32),
+        vm((NS, MSG2, 128), F32),
+        vm((NS, MSG2, 128), F32),
+        vm((NS, MSG1, 128), F32),
+        vm((NS, MSG1, 128), F32),
+        vm((NS, MSG1, 128), F32),
+        vm((NS, MSG1, 128), F32),
         vm((NG, NX, 3, WP, 128), F32),
         vm((2, NB, C, H), jnp.int32),
         vm((2, NB, C, H), jnp.int32),
@@ -491,8 +495,8 @@
         dma((NG,)),
         dma((2,)),
         dma((2,)),
-        dma((3,)),
-        dma((3,)),
+        dma((4,)),
+        dma((4,)),
         dma((NG,)),
         dma((NG,)),
         dma,

time: 172 us -> 168 us (0.977)
  Pallas kernels: 172 us -> 167 us
    pallas_call x1, Pallas kernels: 168 us -> 163 us  [local(): pl.pallas_call(kernel, name='afno_tangent', out_shape=jax.ShapeDtypeStruc...]
where the time goes in v3:
time: 168 us; the launch traced here: 167 us
  Pallas kernels  167 us (99%)
    pallas_call x1, Pallas kernels, local(): pl.pallas_call(kernel, name='afno_tangent', out_shape=jax.ShapeDtypeStruc...  163 us
    pallas_call x1, Pallas kernels, local(): pl.pallas_call(unpack, name='unpack_rows', out_shape=jax.ShapeDtypeStruct...  3.49 us

profile of v3, /device:TPU:1, one launch (start us, length us, event | category | flops | bytes accessed | tf_op | source)
XLA Modules:
  0.0 167.2 jit_solution(11975548097099399245)
XLA Ops:
  0.0 163.5 %afno_tangent.1.packed = f32[3,4,3,184,128]{4,3,2,1,0:T(8,128)} custom-call(f32[45,180,96]{2,1,0:T(8,128)} %fields.1, f32[8,2,96,96]{3,2,1,0:T(8,128)} %w1.1, f32[8,2,96,96]{3,2,1,0:T(8,128)} %w2.1, s32[1,2,8,96,360]{4,3,2,1,0:T(8,128)} %bitcast.2, s32[1,2,8,96,360]{4,3,2,1,0:T(8,128)} %bitcast.3, bf16[2,8,64,768]{3,2,1,0:T(8,128)(2,1)} %constant.8.clone.t_fwd, ...), custom_call_target="tpu_custom_call" | custom-call | tf_op jit(solution)/shard_map/afno_tangent/pallas_call | solution.py:505
  163.5 3.5 %unpack_rows.1 = f32[45,180,96]{2,1,0:T(8,128)} custom-call(f32[3,4,3,184,128]{4,3,2,1,0:T(8,128)} %afno_tangent.1.packed), custom_call_target="tpu_custom_call" | custom-call | tf_op jit(solution)/shard_map/unpack_rows/pallas_call | solution.py:516

commit v4 on v3

--- a/solution.py
+++ b/solution.py
@@ -378,9 +378,6 @@
     send_plane(cs1, cr1, sc, rc, 1)
 
     lat_forward([strided(yr1flat, 4, MSG, 2 + pos) for pos in range(2)])
-    arrived(cr0, rc.at[0])
-    for g in range(NG):
-        add_term(g, [strided(cr0flat, 4, MSG, u) for u in range(4)], (0, 1), first=True)
 
     def put_third(row, pos, value):
         cs2flat[pl.ds(row, NS, stride=MSG1), :] = value
@@ -391,12 +388,15 @@
     arrived(gv.at[pl.ds(0, 2)], rm.at[2])
     lat_back((0,), (mode_at(6),), put_third)
     send_plane(cs2, cr2, sc, rc, 2)
-    arrived(cr1, rc.at[1])
-    for g in range(NG):
-        add_term(g, [strided(cr1flat, 2, MSG2, u) for u in range(2)], (2,))
     arrived(gv.at[pl.ds(0, 2)], rm.at[3])
     lat_back((1,), (mode_at(7),), put_last)
     send_plane(cs3, cr3, sc, rc, 3)
+    arrived(cr0, rc.at[0])
+    for g in range(NG):
+        add_term(g, [strided(cr0flat, 4, MSG, u) for u in range(4)], (0, 1), first=True)
+    arrived(cr1, rc.at[1])
+    for g in range(NG):
+        add_term(g, [strided(cr1flat, 2, MSG2, u) for u in range(2)], (2,))
     arrived(cr2, rc.at[2])
     arrived(cr3, rc.at[3])
     for g in range(NG):

time: 168 us -> 168 us (level)
  no operation moved by 1% of the time
where the time goes in v4:
time: 168 us; the launch traced here: 167 us
  Pallas kernels  167 us (99%)
    pallas_call x1, Pallas kernels, local(): pl.pallas_call(kernel, name='afno_tangent', out_shape=jax.ShapeDtypeStruc...  164 us
    pallas_call x1, Pallas kernels, local(): pl.pallas_call(unpack, name='unpack_rows', out_shape=jax.ShapeDtypeStruct...  3.49 us

profile of v4, /device:TPU:1, one launch (start us, length us, event | category | flops | bytes accessed | tf_op | source)
XLA Modules:
  0.0 167.2 jit_solution(7056096664524150907)
XLA Ops:
  0.0 163.6 %afno_tangent.1.packed = f32[3,4,3,184,128]{4,3,2,1,0:T(8,128)} custom-call(f32[45,180,96]{2,1,0:T(8,128)} %fields.1, f32[8,2,96,96]{3,2,1,0:T(8,128)} %w1.1, f32[8,2,96,96]{3,2,1,0:T(8,128)} %w2.1, s32[1,2,8,96,360]{4,3,2,1,0:T(8,128)} %bitcast.2, s32[1,2,8,96,360]{4,3,2,1,0:T(8,128)} %bitcast.3, bf16[2,8,64,768]{3,2,1,0:T(8,128)(2,1)} %constant.8.clone.t_fwd, ...), custom_call_target="tpu_custom_call" | custom-call | tf_op jit(solution)/shard_map/afno_tangent/pallas_call | solution.py:505
  163.6 3.5 %unpack_rows.1 = f32[45,180,96]{2,1,0:T(8,128)} custom-call(f32[3,4,3,184,128]{4,3,2,1,0:T(8,128)} %afno_tangent.1.packed), custom_call_target="tpu_custom_call" | custom-call | tf_op jit(solution)/shard_map/unpack_rows/pallas_call | solution.py:516
